TPU v7x, 512 devices: a whole 4x8x8 slice. The times are simulated.
512 devices in a mesh: seq: 32 (over z_hi, x, core), head: 16 (over z_lo, y).
Axes of the slice: x: 4, y: 8, z: 8 (z_hi: 4, z_lo: 2; z = z_hi * 2 + z_lo), core: 2. Of those that a mesh axis runs over, the one named last changes fastest.
Arguments:
- queries: bfloat16 [1024, 128, 576], P('seq', 'head'), may hold values from -1024 to 1024
- latents: bfloat16 [4096, 576], P('seq'), may hold values from -6 to 6
- out_grad: bfloat16 [1024, 128, 512], P('seq', 'head'), may hold values from -6 to 6
- layer_out: bfloat16 [1024, 128, 512], P('seq', 'head'), may hold values from -4 to 4
- query_start: int32 [32], P('seq'), may hold values from 0 to 4095, as said below
Outputs:
- query_grad: bfloat16 [1024, 128, 576], P('seq', 'head')
- latent_grad: float32 [4096, 576], P(('seq', 'head'))
Inputs may be any that keep to these rules, and one draw needn't show every extreme that they name: Shard i holds the 32 queries at consecutive positions from query_start[i]; queries past the last latent position see every latent row.
All inputs are finite; a program needn't handle non-finite values.
Results may differ from a plain program's by a relative error of at most 0.0049.
Values may be sent and summed in bfloat16 or wider, within the bound.
No kernel may reach another device: no remote copies, remote signals or barrier semaphores. Data moves between devices by JAX's collectives and lax.ppermute only.
A program may use at most 64 MiB of HBM per device.

v0:
```python
import jax
import jax.numpy as jnp
from jax import lax
from jax.sharding import PartitionSpec as P

score_scale = 192 ** (-0.5)
masked_score = -1e30


def shifted(block, axis, distance):
    devices = range(lax.axis_size(axis))
    route = [((i - distance) % len(devices), i) for i in devices]
    return lax.ppermute(block, axis, route)


def visible_mask(first_key, key_rows, query_pos):
    key_pos = first_key + lax.iota(jnp.int32, key_rows)
    return key_pos[:, None] <= query_pos[None, :]


def score_block(block_rows, query_rows):
    return (
        lax.dot_general(
            block_rows, query_rows, (((1,), (1,)), ((), ())), preferred_element_type=jnp.float32
        )
        * score_scale
    )


def norm_step(running, block_rows, first_row, query_rows, query_pos):
    run_max, run_sum = running
    shown = visible_mask(first_row, block_rows.shape[0], query_pos)
    scores = jnp.where(shown, score_block(block_rows, query_rows), masked_score)
    new_max = jnp.maximum(run_max, jnp.max(scores, axis=0))
    weights = jnp.where(shown, jnp.exp(scores - new_max[None, :]), 0.0)
    run_sum = jnp.sum(weights, axis=0)
    return (new_max, run_sum)


def grad_block(block_rows, first_row, query_rows, grad_rows, row_delta, log_norm, query_pos):
    shown = visible_mask(first_row, block_rows.shape[0], query_pos)
    scores = score_block(block_rows, query_rows)
    weights = jnp.where(
        shown, jnp.exp(jnp.where(shown, scores - log_norm[None, :], masked_score)), 0.0
    )
    value_width = grad_rows.shape[1]
    prob_grad = lax.dot_general(
        block_rows[:, :value_width],
        grad_rows,
        (((1,), (1,)), ((), ())),
        preferred_element_type=jnp.float32,
    )
    dscore = (score_scale * weights * (prob_grad - row_delta[None, :])).astype(jnp.bfloat16)
    key_term = jnp.dot(dscore, query_rows, preferred_element_type=jnp.float32)
    value_term = jnp.dot(
        weights.astype(jnp.bfloat16), grad_rows, preferred_element_type=jnp.float32
    )
    key_term = key_term + jnp.pad(value_term, ((0, 0), (0, block_rows.shape[1] - value_width)))
    query_term = lax.dot_general(
        dscore, block_rows, (((0,), (0,)), ((), ())), preferred_element_type=jnp.float32
    )
    return (key_term, query_term)


def per_device(queries, latents, out_grad, layer_out, query_start):
    query_count, head_count, key_width = queries.shape
    row_count = query_count * head_count
    query_rows = queries.reshape(row_count, key_width)
    grad_rows = out_grad.reshape(row_count, out_grad.shape[2])
    row_delta = jnp.sum(
        out_grad.astype(jnp.float32) * layer_out.astype(jnp.float32), axis=2
    ).reshape(row_count)
    query_pos = query_start[0] + lax.iota(jnp.int32, row_count) // head_count
    key_count = latents.shape[0]
    cycle_size = lax.axis_size("seq")
    my_index = lax.axis_index("seq")
    start_state = (
        jnp.full((row_count,), masked_score, jnp.float32),
        jnp.zeros((row_count,), jnp.float32),
    )
    block_rows = lax.all_gather(latents, "seq", axis=0, tiled=True)
    running = start_state
    running = norm_step(running, block_rows, jnp.int32(0), query_rows, query_pos)
    add_stored = block_rows
    (run_max, run_sum), stored = (running, add_stored)
    log_norm = run_max + jnp.log(run_sum)

    def visit(first_row, rows, grad_sum, query_sum):
        block_rows = lax.dynamic_slice_in_dim(stored, first_row, rows, 0)
        key_term, query_term = grad_block(
            block_rows, first_row, query_rows, grad_rows, row_delta, log_norm, query_pos
        )
        return (grad_sum + key_term, query_sum + query_term)

    query_start_sum = jnp.zeros((row_count, key_width), jnp.float32)

    def cycle_turn(turn_index, state):
        grad_sum, query_sum = state
        owner_index = (my_index - turn_index - 1) % cycle_size
        grad_sum, query_sum = visit(owner_index * key_count, key_count, grad_sum, query_sum)
        return (shifted(grad_sum, "seq", 1), query_sum)

    start_sum = jnp.zeros((key_count, key_width), jnp.float32)
    grad_sum, query_sum = lax.fori_loop(0, cycle_size - 1, cycle_turn, (start_sum, query_start_sum))
    owned_sum, query_sum = visit(my_index * key_count, key_count, grad_sum, query_sum)
    latent_grad = lax.psum_scatter(owned_sum, "head", scatter_dimension=0, tiled=True)
    query_grad = query_sum.astype(jnp.bfloat16).reshape(query_count, head_count, key_width)
    return (query_grad, latent_grad)


def solution(mesh):
    placed = (
        P("seq", "head", None),
        P("seq", None),
        P("seq", "head", None),
        P("seq", "head", None),
        P("seq"),
    )
    return jax.shard_map(
        per_device,
        mesh=mesh,
        in_specs=placed,
        out_specs=(P("seq", "head", None), P(("seq", "head"), None)),
        check_vma=False,
    )
```

profile of v0, /device:TPU:2, one launch (start us, length us, event | category | flops | bytes accessed | tf_op | source)
XLA Modules:
  0.0 738.1 jit_solution(2161569260429799532)
XLA Ops:
  11.1 75.9 %all-gather.2.cloned.1.call-done = bf16[4096,576]{1,0:T(8,128)(2,1)} async-done(((bf16[128,576]{1,0:T(8,128)(2,1)}), bf16[4096,576]{1,0:T(8,128)(2,1)}) %all-gather.2.cloned.1.call-update) | async-done | bytes 4718608 | tf_op jit(solution)/shard_map/all_gather | solution.py:81
  87.0 4.4 fusion.41
  94.0 479.8 %while.19 = (s32[]{:T(128)}, f32[128,576]{0,1:T(8,128)S(1)}, f32[256,576]{0,1:T(8,128)S(1)}, s32[]{:T(128)}, bf16[4096,576]{1,0:T(8,128)(2,1)}, /*index=5*/bf16[...) while((s32[]{:T(128)}, f32[128,576]{0,1:T(8,128)S(1)}, ...), condition=%wide.wide.region_4.5_spmd.clone, body=%wide.wide.region_3.4_spmd.clone.sunk | while | flops 181127568 | bytes 5641630 | solution.py:104
  97.6 2.2 collective-permute-start
  101.1 4.6 collective-permute-done
  109.2 1.9 collective-permute-start
  112.4 4.8 collective-permute-done
  120.9 1.9 collective-permute-start
  124.1 4.8 collective-permute-done
  132.5 1.9 collective-permute-start
  135.7 8.6 %collective-permute-done = f32[128,576]{0,1:T(8,128)S(1)} collective-permute-done((f32[128,576]{0,1:T(8,128)S(1)}, f32[128,576]{0,1:T(8,128)S(1)}, u32[]{:S(2)}, u32[]{:S(2)}) %collective-permute-start) | collective-permute-done | bytes 294944 | tf_op jit(solution)/shard_map/while/body/eval_jaxpr/ppermute | solution.py:13
  147.9 1.9 collective-permute-start
  151.1 9.0 %collective-permute-done = f32[128,576]{0,1:T(8,128)S(1)} collective-permute-done((f32[128,576]{0,1:T(8,128)S(1)}, f32[128,576]{0,1:T(8,128)S(1)}, u32[]{:S(2)}, u32[]{:S(2)}) %collective-permute-start) | collective-permute-done | bytes 294944 | tf_op jit(solution)/shard_map/while/body/eval_jaxpr/ppermute | solution.py:13
  163.7 1.9 collective-permute-start
  167.0 9.0 %collective-permute-done = f32[128,576]{0,1:T(8,128)S(1)} collective-permute-done((f32[128,576]{0,1:T(8,128)S(1)}, f32[128,576]{0,1:T(8,128)S(1)}, u32[]{:S(2)}, u32[]{:S(2)}) %collective-permute-start) | collective-permute-done | bytes 294944 | tf_op jit(solution)/shard_map/while/body/eval_jaxpr/ppermute | solution.py:13
  179.6 1.9 collective-permute-start
  182.8 9.0 %collective-permute-done = f32[128,576]{0,1:T(8,128)S(1)} collective-permute-done((f32[128,576]{0,1:T(8,128)S(1)}, f32[128,576]{0,1:T(8,128)S(1)}, u32[]{:S(2)}, u32[]{:S(2)}) %collective-permute-start) | collective-permute-done | bytes 294944 | tf_op jit(solution)/shard_map/while/body/eval_jaxpr/ppermute | solution.py:13
  195.4 1.9 collective-permute-start
  198.7 9.0 %collective-permute-done = f32[128,576]{0,1:T(8,128)S(1)} collective-permute-done((f32[128,576]{0,1:T(8,128)S(1)}, f32[128,576]{0,1:T(8,128)S(1)}, u32[]{:S(2)}, u32[]{:S(2)}) %collective-permute-start) | collective-permute-done | bytes 294944 | tf_op jit(solution)/shard_map/while/body/eval_jaxpr/ppermute | solution.py:13
  211.3 1.9 collective-permute-start
  214.5 9.0 %collective-permute-done = f32[128,576]{0,1:T(8,128)S(1)} collective-permute-done((f32[128,576]{0,1:T(8,128)S(1)}, f32[128,576]{0,1:T(8,128)S(1)}, u32[]{:S(2)}, u32[]{:S(2)}) %collective-permute-start) | collective-permute-done | bytes 294944 | tf_op jit(solution)/shard_map/while/body/eval_jaxpr/ppermute | solution.py:13
  227.1 1.9 collective-permute-start
  230.3 9.0 %collective-permute-done = f32[128,576]{0,1:T(8,128)S(1)} collective-permute-done((f32[128,576]{0,1:T(8,128)S(1)}, f32[128,576]{0,1:T(8,128)S(1)}, u32[]{:S(2)}, u32[]{:S(2)}) %collective-permute-start) | collective-permute-done | bytes 294944 | tf_op jit(solution)/shard_map/while/body/eval_jaxpr/ppermute | solution.py:13
  243.0 1.9 collective-permute-start
  246.2 9.0 %collective-permute-done = f32[128,576]{0,1:T(8,128)S(1)} collective-permute-done((f32[128,576]{0,1:T(8,128)S(1)}, f32[128,576]{0,1:T(8,128)S(1)}, u32[]{:S(2)}, u32[]{:S(2)}) %collective-permute-start) | collective-permute-done | bytes 294944 | tf_op jit(solution)/shard_map/while/body/eval_jaxpr/ppermute | solution.py:13
  258.8 1.9 collective-permute-start
  262.0 9.0 %collective-permute-done = f32[128,576]{0,1:T(8,128)S(1)} collective-permute-done((f32[128,576]{0,1:T(8,128)S(1)}, f32[128,576]{0,1:T(8,128)S(1)}, u32[]{:S(2)}, u32[]{:S(2)}) %collective-permute-start) | collective-permute-done | bytes 294944 | tf_op jit(solution)/shard_map/while/body/eval_jaxpr/ppermute | solution.py:13
  274.6 1.9 collective-permute-start
  277.9 9.0 %collective-permute-done = f32[128,576]{0,1:T(8,128)S(1)} collective-permute-done((f32[128,576]{0,1:T(8,128)S(1)}, f32[128,576]{0,1:T(8,128)S(1)}, u32[]{:S(2)}, u32[]{:S(2)}) %collective-permute-start) | collective-permute-done | bytes 294944 | tf_op jit(solution)/shard_map/while/body/eval_jaxpr/ppermute | solution.py:13
  290.5 1.9 collective-permute-start
  293.7 9.0 %collective-permute-done = f32[128,576]{0,1:T(8,128)S(1)} collective-permute-done((f32[128,576]{0,1:T(8,128)S(1)}, f32[128,576]{0,1:T(8,128)S(1)}, u32[]{:S(2)}, u32[]{:S(2)}) %collective-permute-start) | collective-permute-done | bytes 294944 | tf_op jit(solution)/shard_map/while/body/eval_jaxpr/ppermute | solution.py:13
  306.3 1.9 collective-permute-start
  309.5 9.1 %collective-permute-done = f32[128,576]{0,1:T(8,128)S(1)} collective-permute-done((f32[128,576]{0,1:T(8,128)S(1)}, f32[128,576]{0,1:T(8,128)S(1)}, u32[]{:S(2)}, u32[]{:S(2)}) %collective-permute-start) | collective-permute-done | bytes 294944 | tf_op jit(solution)/shard_map/while/body/eval_jaxpr/ppermute | solution.py:13
  322.3 1.9 collective-permute-start
  325.5 9.1 %collective-permute-done = f32[128,576]{0,1:T(8,128)S(1)} collective-permute-done((f32[128,576]{0,1:T(8,128)S(1)}, f32[128,576]{0,1:T(8,128)S(1)}, u32[]{:S(2)}, u32[]{:S(2)}) %collective-permute-start) | collective-permute-done | bytes 294944 | tf_op jit(solution)/shard_map/while/body/eval_jaxpr/ppermute | solution.py:13
  338.2 1.9 collective-permute-start
  341.4 9.1 %collective-permute-done = f32[128,576]{0,1:T(8,128)S(1)} collective-permute-done((f32[128,576]{0,1:T(8,128)S(1)}, f32[128,576]{0,1:T(8,128)S(1)}, u32[]{:S(2)}, u32[]{:S(2)}) %collective-permute-start) | collective-permute-done | bytes 294944 | tf_op jit(solution)/shard_map/while/body/eval_jaxpr/ppermute | solution.py:13
  354.1 1.9 collective-permute-start
  357.4 9.1 %collective-permute-done = f32[128,576]{0,1:T(8,128)S(1)} collective-permute-done((f32[128,576]{0,1:T(8,128)S(1)}, f32[128,576]{0,1:T(8,128)S(1)}, u32[]{:S(2)}, u32[]{:S(2)}) %collective-permute-start) | collective-permute-done | bytes 294944 | tf_op jit(solution)/shard_map/while/body/eval_jaxpr/ppermute | solution.py:13
  370.1 1.9 collective-permute-start
  373.3 9.1 %collective-permute-done = f32[128,576]{0,1:T(8,128)S(1)} collective-permute-done((f32[128,576]{0,1:T(8,128)S(1)}, f32[128,576]{0,1:T(8,128)S(1)}, u32[]{:S(2)}, u32[]{:S(2)}) %collective-permute-start) | collective-permute-done | bytes 294944 | tf_op jit(solution)/shard_map/while/body/eval_jaxpr/ppermute | solution.py:13
  386.0 1.9 collective-permute-start
  389.2 9.1 %collective-permute-done = f32[128,576]{0,1:T(8,128)S(1)} collective-permute-done((f32[128,576]{0,1:T(8,128)S(1)}, f32[128,576]{0,1:T(8,128)S(1)}, u32[]{:S(2)}, u32[]{:S(2)}) %collective-permute-start) | collective-permute-done | bytes 294944 | tf_op jit(solution)/shard_map/while/body/eval_jaxpr/ppermute | solution.py:13
  402.0 1.9 collective-permute-start
  405.2 9.1 %collective-permute-done = f32[128,576]{0,1:T(8,128)S(1)} collective-permute-done((f32[128,576]{0,1:T(8,128)S(1)}, f32[128,576]{0,1:T(8,128)S(1)}, u32[]{:S(2)}, u32[]{:S(2)}) %collective-permute-start) | collective-permute-done | bytes 294944 | tf_op jit(solution)/shard_map/while/body/eval_jaxpr/ppermute | solution.py:13
  417.9 1.9 collective-permute-start
  421.1 9.1 %collective-permute-done = f32[128,576]{0,1:T(8,128)S(1)} collective-permute-done((f32[128,576]{0,1:T(8,128)S(1)}, f32[128,576]{0,1:T(8,128)S(1)}, u32[]{:S(2)}, u32[]{:S(2)}) %collective-permute-start) | collective-permute-done | bytes 294944 | tf_op jit(solution)/shard_map/while/body/eval_jaxpr/ppermute | solution.py:13
  433.8 1.9 collective-permute-start
  437.1 9.1 %collective-permute-done = f32[128,576]{0,1:T(8,128)S(1)} collective-permute-done((f32[128,576]{0,1:T(8,128)S(1)}, f32[128,576]{0,1:T(8,128)S(1)}, u32[]{:S(2)}, u32[]{:S(2)}) %collective-permute-start) | collective-permute-done | bytes 294944 | tf_op jit(solution)/shard_map/while/body/eval_jaxpr/ppermute | solution.py:13
  449.8 1.9 collective-permute-start
  453.0 9.1 %collective-permute-done = f32[128,576]{0,1:T(8,128)S(1)} collective-permute-done((f32[128,576]{0,1:T(8,128)S(1)}, f32[128,576]{0,1:T(8,128)S(1)}, u32[]{:S(2)}, u32[]{:S(2)}) %collective-permute-start) | collective-permute-done | bytes 294944 | tf_op jit(solution)/shard_map/while/body/eval_jaxpr/ppermute | solution.py:13
  465.7 1.9 collective-permute-start
  468.9 9.1 %collective-permute-done = f32[128,576]{0,1:T(8,128)S(1)} collective-permute-done((f32[128,576]{0,1:T(8,128)S(1)}, f32[128,576]{0,1:T(8,128)S(1)}, u32[]{:S(2)}, u32[]{:S(2)}) %collective-permute-start) | collective-permute-done | bytes 294944 | tf_op jit(solution)/shard_map/while/body/eval_jaxpr/ppermute | solution.py:13
  481.7 1.9 collective-permute-start
  484.9 9.1 %collective-permute-done = f32[128,576]{0,1:T(8,128)S(1)} collective-permute-done((f32[128,576]{0,1:T(8,128)S(1)}, f32[128,576]{0,1:T(8,128)S(1)}, u32[]{:S(2)}, u32[]{:S(2)}) %collective-permute-start) | collective-permute-done | bytes 294944 | tf_op jit(solution)/shard_map/while/body/eval_jaxpr/ppermute | solution.py:13
  497.6 1.9 collective-permute-start
  500.8 9.1 %collective-permute-done = f32[128,576]{0,1:T(8,128)S(1)} collective-permute-done((f32[128,576]{0,1:T(8,128)S(1)}, f32[128,576]{0,1:T(8,128)S(1)}, u32[]{:S(2)}, u32[]{:S(2)}) %collective-permute-start) | collective-permute-done | bytes 294944 | tf_op jit(solution)/shard_map/while/body/eval_jaxpr/ppermute | solution.py:13
  513.6 1.9 collective-permute-start
  516.8 9.1 %collective-permute-done = f32[128,576]{0,1:T(8,128)S(1)} collective-permute-done((f32[128,576]{0,1:T(8,128)S(1)}, f32[128,576]{0,1:T(8,128)S(1)}, u32[]{:S(2)}, u32[]{:S(2)}) %collective-permute-start) | collective-permute-done | bytes 294944 | tf_op jit(solution)/shard_map/while/body/eval_jaxpr/ppermute | solution.py:13
  529.5 1.9 collective-permute-start
  532.7 9.1 %collective-permute-done = f32[128,576]{0,1:T(8,128)S(1)} collective-permute-done((f32[128,576]{0,1:T(8,128)S(1)}, f32[128,576]{0,1:T(8,128)S(1)}, u32[]{:S(2)}, u32[]{:S(2)}) %collective-permute-start) | collective-permute-done | bytes 294944 | tf_op jit(solution)/shard_map/while/body/eval_jaxpr/ppermute | solution.py:13
  548.7 9.1 %collective-permute-done = f32[128,576]{0,1:T(8,128)S(1)} collective-permute-done((f32[128,576]{0,1:T(8,128)S(1)}, f32[128,576]{0,1:T(8,128)S(1)}, u32[]{:S(2)}, u32[]{:S(2)}) %collective-permute-start) | collective-permute-done | bytes 294944 | tf_op jit(solution)/shard_map/while/body/eval_jaxpr/ppermute | solution.py:13
  564.6 9.1 %collective-permute-done = f32[128,576]{0,1:T(8,128)S(1)} collective-permute-done((f32[128,576]{0,1:T(8,128)S(1)}, f32[128,576]{0,1:T(8,128)S(1)}, u32[]{:S(2)}, u32[]{:S(2)}) %collective-permute-start) | collective-permute-done | bytes 294944 | tf_op jit(solution)/shard_map/while/body/eval_jaxpr/ppermute | solution.py:13
  580.1 149.8 %all-reduce.5.cloned.1.call-done = f32[128,576]{1,0:T(8,128)} async-done(((f32[128,576]{1,0:T(8,128)}), f32[128,576]{1,0:T(8,128)}) %all-reduce.5.cloned.1.call-update) | async-done | bytes 294928
  (249 shorter events, 166.1 us)
Async XLA Ops:
  7.2 79.9 %all-gather.2.cloned.1.call-start = ((), (), s32[]{:S(2)}) async-start(), calls=%async_computation | async-start | bytes 5406720 | tf_op jit(solution)/shard_map/all_gather | solution.py:81
  8.9 720.9 %all-reduce.5.cloned.1.call-start = ((), (), s32[]{:S(2)}) async-start(), calls=%async_computation.1 | async-start | bytes 655360
  10.2 81.2 %copy-start.2 = (f32[32,8]{1,0:T(8,128)}, f32[32,8]{1,0:T(8,128)S(1)}, u32[]{:S(2)}) copy-start(f32[32,8]{1,0:T(8,128)S(1)} %multiply_reduce_fusion) | copy-start | bytes 3076
  11.1 81.5 %copy-start = (bf16[32,8,576]{2,1,0:T(8,128)(2,1)S(1)}, bf16[32,8,576]{2,1,0:T(8,128)(2,1)}, u32[]{:S(2)}) copy-start(bf16[32,8,576]{2,1,0:T(8,128)(2,1)} %param.7) | copy-start | bytes 884740
  11.1 82.7 %copy-start.1 = (bf16[32,8,512]{2,1,0:T(8,128)(2,1)S(1)}, bf16[32,8,512]{2,1,0:T(8,128)(2,1)}, u32[]{:S(2)}) copy-start(bf16[32,8,512]{2,1,0:T(8,128)(2,1)} %param.9) | copy-start | bytes 786436
  97.6 8.0 %collective-permute-start = (f32[128,576]{0,1:T(8,128)S(1)}, f32[128,576]{0,1:T(8,128)S(1)}, u32[]{:S(2)}, u32[]{:S(2)}) collective-permute-start(f32[128,576]{0,1:T(8,128)S(1)} %fusion.95), channel_id=1, source_target_pairs={{496,0},{0,16},{16,32},{32,48},{48,64},{64,80},{80,96},{96,112},{1... | collective-permute-start | bytes 884744 | tf_op jit(solution)/shard_map/while/body/eval_jaxpr/ppermute | solution.py:13
  109.2 8.0 %collective-permute-start = (f32[128,576]{0,1:T(8,128)S(1)}, f32[128,576]{0,1:T(8,128)S(1)}, u32[]{:S(2)}, u32[]{:S(2)}) collective-permute-start(f32[128,576]{0,1:T(8,128)S(1)} %fusion.95), channel_id=1, source_target_pairs={{496,0},{0,16},{16,32},{32,48},{48,64},{64,80},{80,96},{96,112},{1... | collective-permute-start | bytes 884744 | tf_op jit(solution)/shard_map/while/body/eval_jaxpr/ppermute | solution.py:13
  120.9 8.0 %collective-permute-start = (f32[128,576]{0,1:T(8,128)S(1)}, f32[128,576]{0,1:T(8,128)S(1)}, u32[]{:S(2)}, u32[]{:S(2)}) collective-permute-start(f32[128,576]{0,1:T(8,128)S(1)} %fusion.95), channel_id=1, source_target_pairs={{496,0},{0,16},{16,32},{32,48},{48,64},{64,80},{80,96},{96,112},{1... | collective-permute-start | bytes 884744 | tf_op jit(solution)/shard_map/while/body/eval_jaxpr/ppermute | solution.py:13
  132.5 11.8 %collective-permute-start = (f32[128,576]{0,1:T(8,128)S(1)}, f32[128,576]{0,1:T(8,128)S(1)}, u32[]{:S(2)}, u32[]{:S(2)}) collective-permute-start(f32[128,576]{0,1:T(8,128)S(1)} %fusion.95), channel_id=1, source_target_pairs={{496,0},{0,16},{16,32},{32,48},{48,64},{64,80},{80,96},{96,112},{1... | collective-permute-start | bytes 884744 | tf_op jit(solution)/shard_map/while/body/eval_jaxpr/ppermute | solution.py:13
  147.9 12.3 %collective-permute-start = (f32[128,576]{0,1:T(8,128)S(1)}, f32[128,576]{0,1:T(8,128)S(1)}, u32[]{:S(2)}, u32[]{:S(2)}) collective-permute-start(f32[128,576]{0,1:T(8,128)S(1)} %fusion.95), channel_id=1, source_target_pairs={{496,0},{0,16},{16,32},{32,48},{48,64},{64,80},{80,96},{96,112},{1... | collective-permute-start | bytes 884744 | tf_op jit(solution)/shard_map/while/body/eval_jaxpr/ppermute | solution.py:13
  163.7 12.3 %collective-permute-start = (f32[128,576]{0,1:T(8,128)S(1)}, f32[128,576]{0,1:T(8,128)S(1)}, u32[]{:S(2)}, u32[]{:S(2)}) collective-permute-start(f32[128,576]{0,1:T(8,128)S(1)} %fusion.95), channel_id=1, source_target_pairs={{496,0},{0,16},{16,32},{32,48},{48,64},{64,80},{80,96},{96,112},{1... | collective-permute-start | bytes 884744 | tf_op jit(solution)/shard_map/while/body/eval_jaxpr/ppermute | solution.py:13
  179.6 12.3 %collective-permute-start = (f32[128,576]{0,1:T(8,128)S(1)}, f32[128,576]{0,1:T(8,128)S(1)}, u32[]{:S(2)}, u32[]{:S(2)}) collective-permute-start(f32[128,576]{0,1:T(8,128)S(1)} %fusion.95), channel_id=1, source_target_pairs={{496,0},{0,16},{16,32},{32,48},{48,64},{64,80},{80,96},{96,112},{1... | collective-permute-start | bytes 884744 | tf_op jit(solution)/shard_map/while/body/eval_jaxpr/ppermute | solution.py:13
  195.4 12.3 %collective-permute-start = (f32[128,576]{0,1:T(8,128)S(1)}, f32[128,576]{0,1:T(8,128)S(1)}, u32[]{:S(2)}, u32[]{:S(2)}) collective-permute-start(f32[128,576]{0,1:T(8,128)S(1)} %fusion.95), channel_id=1, source_target_pairs={{496,0},{0,16},{16,32},{32,48},{48,64},{64,80},{80,96},{96,112},{1... | collective-permute-start | bytes 884744 | tf_op jit(solution)/shard_map/while/body/eval_jaxpr/ppermute | solution.py:13
  211.3 12.3 %collective-permute-start = (f32[128,576]{0,1:T(8,128)S(1)}, f32[128,576]{0,1:T(8,128)S(1)}, u32[]{:S(2)}, u32[]{:S(2)}) collective-permute-start(f32[128,576]{0,1:T(8,128)S(1)} %fusion.95), channel_id=1, source_target_pairs={{496,0},{0,16},{16,32},{32,48},{48,64},{64,80},{80,96},{96,112},{1... | collective-permute-start | bytes 884744 | tf_op jit(solution)/shard_map/while/body/eval_jaxpr/ppermute | solution.py:13
  227.1 12.3 %collective-permute-start = (f32[128,576]{0,1:T(8,128)S(1)}, f32[128,576]{0,1:T(8,128)S(1)}, u32[]{:S(2)}, u32[]{:S(2)}) collective-permute-start(f32[128,576]{0,1:T(8,128)S(1)} %fusion.95), channel_id=1, source_target_pairs={{496,0},{0,16},{16,32},{32,48},{48,64},{64,80},{80,96},{96,112},{1... | collective-permute-start | bytes 884744 | tf_op jit(solution)/shard_map/while/body/eval_jaxpr/ppermute | solution.py:13
  243.0 12.3 %collective-permute-start = (f32[128,576]{0,1:T(8,128)S(1)}, f32[128,576]{0,1:T(8,128)S(1)}, u32[]{:S(2)}, u32[]{:S(2)}) collective-permute-start(f32[128,576]{0,1:T(8,128)S(1)} %fusion.95), channel_id=1, source_target_pairs={{496,0},{0,16},{16,32},{32,48},{48,64},{64,80},{80,96},{96,112},{1... | collective-permute-start | bytes 884744 | tf_op jit(solution)/shard_map/while/body/eval_jaxpr/ppermute | solution.py:13
  258.8 12.3 %collective-permute-start = (f32[128,576]{0,1:T(8,128)S(1)}, f32[128,576]{0,1:T(8,128)S(1)}, u32[]{:S(2)}, u32[]{:S(2)}) collective-permute-start(f32[128,576]{0,1:T(8,128)S(1)} %fusion.95), channel_id=1, source_target_pairs={{496,0},{0,16},{16,32},{32,48},{48,64},{64,80},{80,96},{96,112},{1... | collective-permute-start | bytes 884744 | tf_op jit(solution)/shard_map/while/body/eval_jaxpr/ppermute | solution.py:13
  274.6 12.3 %collective-permute-start = (f32[128,576]{0,1:T(8,128)S(1)}, f32[128,576]{0,1:T(8,128)S(1)}, u32[]{:S(2)}, u32[]{:S(2)}) collective-permute-start(f32[128,576]{0,1:T(8,128)S(1)} %fusion.95), channel_id=1, source_target_pairs={{496,0},{0,16},{16,32},{32,48},{48,64},{64,80},{80,96},{96,112},{1... | collective-permute-start | bytes 884744 | tf_op jit(solution)/shard_map/while/body/eval_jaxpr/ppermute | solution.py:13
  290.5 12.3 %collective-permute-start = (f32[128,576]{0,1:T(8,128)S(1)}, f32[128,576]{0,1:T(8,128)S(1)}, u32[]{:S(2)}, u32[]{:S(2)}) collective-permute-start(f32[128,576]{0,1:T(8,128)S(1)} %fusion.95), channel_id=1, source_target_pairs={{496,0},{0,16},{16,32},{32,48},{48,64},{64,80},{80,96},{96,112},{1... | collective-permute-start | bytes 884744 | tf_op jit(solution)/shard_map/while/body/eval_jaxpr/ppermute | solution.py:13
  306.3 12.3 %collective-permute-start = (f32[128,576]{0,1:T(8,128)S(1)}, f32[128,576]{0,1:T(8,128)S(1)}, u32[]{:S(2)}, u32[]{:S(2)}) collective-permute-start(f32[128,576]{0,1:T(8,128)S(1)} %fusion.95), channel_id=1, source_target_pairs={{496,0},{0,16},{16,32},{32,48},{48,64},{64,80},{80,96},{96,112},{1... | collective-permute-start | bytes 884744 | tf_op jit(solution)/shard_map/while/body/eval_jaxpr/ppermute | solution.py:13
  322.3 12.4 %collective-permute-start = (f32[128,576]{0,1:T(8,128)S(1)}, f32[128,576]{0,1:T(8,128)S(1)}, u32[]{:S(2)}, u32[]{:S(2)}) collective-permute-start(f32[128,576]{0,1:T(8,128)S(1)} %fusion.95), channel_id=1, source_target_pairs={{496,0},{0,16},{16,32},{32,48},{48,64},{64,80},{80,96},{96,112},{1... | collective-permute-start | bytes 884744 | tf_op jit(solution)/shard_map/while/body/eval_jaxpr/ppermute | solution.py:13
  338.2 12.4 %collective-permute-start = (f32[128,576]{0,1:T(8,128)S(1)}, f32[128,576]{0,1:T(8,128)S(1)}, u32[]{:S(2)}, u32[]{:S(2)}) collective-permute-start(f32[128,576]{0,1:T(8,128)S(1)} %fusion.95), channel_id=1, source_target_pairs={{496,0},{0,16},{16,32},{32,48},{48,64},{64,80},{80,96},{96,112},{1... | collective-permute-start | bytes 884744 | tf_op jit(solution)/shard_map/while/body/eval_jaxpr/ppermute | solution.py:13
  354.1 12.4 %collective-permute-start = (f32[128,576]{0,1:T(8,128)S(1)}, f32[128,576]{0,1:T(8,128)S(1)}, u32[]{:S(2)}, u32[]{:S(2)}) collective-permute-start(f32[128,576]{0,1:T(8,128)S(1)} %fusion.95), channel_id=1, source_target_pairs={{496,0},{0,16},{16,32},{32,48},{48,64},{64,80},{80,96},{96,112},{1... | collective-permute-start | bytes 884744 | tf_op jit(solution)/shard_map/while/body/eval_jaxpr/ppermute | solution.py:13
  370.1 12.4 %collective-permute-start = (f32[128,576]{0,1:T(8,128)S(1)}, f32[128,576]{0,1:T(8,128)S(1)}, u32[]{:S(2)}, u32[]{:S(2)}) collective-permute-start(f32[128,576]{0,1:T(8,128)S(1)} %fusion.95), channel_id=1, source_target_pairs={{496,0},{0,16},{16,32},{32,48},{48,64},{64,80},{80,96},{96,112},{1... | collective-permute-start | bytes 884744 | tf_op jit(solution)/shard_map/while/body/eval_jaxpr/ppermute | solution.py:13
  386.0 12.4 %collective-permute-start = (f32[128,576]{0,1:T(8,128)S(1)}, f32[128,576]{0,1:T(8,128)S(1)}, u32[]{:S(2)}, u32[]{:S(2)}) collective-permute-start(f32[128,576]{0,1:T(8,128)S(1)} %fusion.95), channel_id=1, source_target_pairs={{496,0},{0,16},{16,32},{32,48},{48,64},{64,80},{80,96},{96,112},{1... | collective-permute-start | bytes 884744 | tf_op jit(solution)/shard_map/while/body/eval_jaxpr/ppermute | solution.py:13
  402.0 12.4 %collective-permute-start = (f32[128,576]{0,1:T(8,128)S(1)}, f32[128,576]{0,1:T(8,128)S(1)}, u32[]{:S(2)}, u32[]{:S(2)}) collective-permute-start(f32[128,576]{0,1:T(8,128)S(1)} %fusion.95), channel_id=1, source_target_pairs={{496,0},{0,16},{16,32},{32,48},{48,64},{64,80},{80,96},{96,112},{1... | collective-permute-start | bytes 884744 | tf_op jit(solution)/shard_map/while/body/eval_jaxpr/ppermute | solution.py:13
  417.9 12.4 %collective-permute-start = (f32[128,576]{0,1:T(8,128)S(1)}, f32[128,576]{0,1:T(8,128)S(1)}, u32[]{:S(2)}, u32[]{:S(2)}) collective-permute-start(f32[128,576]{0,1:T(8,128)S(1)} %fusion.95), channel_id=1, source_target_pairs={{496,0},{0,16},{16,32},{32,48},{48,64},{64,80},{80,96},{96,112},{1... | collective-permute-start | bytes 884744 | tf_op jit(solution)/shard_map/while/body/eval_jaxpr/ppermute | solution.py:13
  433.8 12.4 %collective-permute-start = (f32[128,576]{0,1:T(8,128)S(1)}, f32[128,576]{0,1:T(8,128)S(1)}, u32[]{:S(2)}, u32[]{:S(2)}) collective-permute-start(f32[128,576]{0,1:T(8,128)S(1)} %fusion.95), channel_id=1, source_target_pairs={{496,0},{0,16},{16,32},{32,48},{48,64},{64,80},{80,96},{96,112},{1... | collective-permute-start | bytes 884744 | tf_op jit(solution)/shard_map/while/body/eval_jaxpr/ppermute | solution.py:13
  449.8 12.4 %collective-permute-start = (f32[128,576]{0,1:T(8,128)S(1)}, f32[128,576]{0,1:T(8,128)S(1)}, u32[]{:S(2)}, u32[]{:S(2)}) collective-permute-start(f32[128,576]{0,1:T(8,128)S(1)} %fusion.95), channel_id=1, source_target_pairs={{496,0},{0,16},{16,32},{32,48},{48,64},{64,80},{80,96},{96,112},{1... | collective-permute-start | bytes 884744 | tf_op jit(solution)/shard_map/while/body/eval_jaxpr/ppermute | solution.py:13
  465.7 12.4 %collective-permute-start = (f32[128,576]{0,1:T(8,128)S(1)}, f32[128,576]{0,1:T(8,128)S(1)}, u32[]{:S(2)}, u32[]{:S(2)}) collective-permute-start(f32[128,576]{0,1:T(8,128)S(1)} %fusion.95), channel_id=1, source_target_pairs={{496,0},{0,16},{16,32},{32,48},{48,64},{64,80},{80,96},{96,112},{1... | collective-permute-start | bytes 884744 | tf_op jit(solution)/shard_map/while/body/eval_jaxpr/ppermute | solution.py:13
  481.7 12.4 %collective-permute-start = (f32[128,576]{0,1:T(8,128)S(1)}, f32[128,576]{0,1:T(8,128)S(1)}, u32[]{:S(2)}, u32[]{:S(2)}) collective-permute-start(f32[128,576]{0,1:T(8,128)S(1)} %fusion.95), channel_id=1, source_target_pairs={{496,0},{0,16},{16,32},{32,48},{48,64},{64,80},{80,96},{96,112},{1... | collective-permute-start | bytes 884744 | tf_op jit(solution)/shard_map/while/body/eval_jaxpr/ppermute | solution.py:13
  497.6 12.4 %collective-permute-start = (f32[128,576]{0,1:T(8,128)S(1)}, f32[128,576]{0,1:T(8,128)S(1)}, u32[]{:S(2)}, u32[]{:S(2)}) collective-permute-start(f32[128,576]{0,1:T(8,128)S(1)} %fusion.95), channel_id=1, source_target_pairs={{496,0},{0,16},{16,32},{32,48},{48,64},{64,80},{80,96},{96,112},{1... | collective-permute-start | bytes 884744 | tf_op jit(solution)/shard_map/while/body/eval_jaxpr/ppermute | solution.py:13
  513.6 12.4 %collective-permute-start = (f32[128,576]{0,1:T(8,128)S(1)}, f32[128,576]{0,1:T(8,128)S(1)}, u32[]{:S(2)}, u32[]{:S(2)}) collective-permute-start(f32[128,576]{0,1:T(8,128)S(1)} %fusion.95), channel_id=1, source_target_pairs={{496,0},{0,16},{16,32},{32,48},{48,64},{64,80},{80,96},{96,112},{1... | collective-permute-start | bytes 884744 | tf_op jit(solution)/shard_map/while/body/eval_jaxpr/ppermute | solution.py:13
  529.5 12.4 %collective-permute-start = (f32[128,576]{0,1:T(8,128)S(1)}, f32[128,576]{0,1:T(8,128)S(1)}, u32[]{:S(2)}, u32[]{:S(2)}) collective-permute-start(f32[128,576]{0,1:T(8,128)S(1)} %fusion.95), channel_id=1, source_target_pairs={{496,0},{0,16},{16,32},{32,48},{48,64},{64,80},{80,96},{96,112},{1... | collective-permute-start | bytes 884744 | tf_op jit(solution)/shard_map/while/body/eval_jaxpr/ppermute | solution.py:13
  545.4 12.4 %collective-permute-start = (f32[128,576]{0,1:T(8,128)S(1)}, f32[128,576]{0,1:T(8,128)S(1)}, u32[]{:S(2)}, u32[]{:S(2)}) collective-permute-start(f32[128,576]{0,1:T(8,128)S(1)} %fusion.95), channel_id=1, source_target_pairs={{496,0},{0,16},{16,32},{32,48},{48,64},{64,80},{80,96},{96,112},{1... | collective-permute-start | bytes 884744 | tf_op jit(solution)/shard_map/while/body/eval_jaxpr/ppermute | solution.py:13
  561.4 12.4 %collective-permute-start = (f32[128,576]{0,1:T(8,128)S(1)}, f32[128,576]{0,1:T(8,128)S(1)}, u32[]{:S(2)}, u32[]{:S(2)}) collective-permute-start(f32[128,576]{0,1:T(8,128)S(1)} %fusion.95), channel_id=1, source_target_pairs={{496,0},{0,16},{16,32},{32,48},{48,64},{64,80},{80,96},{96,112},{1... | collective-permute-start | bytes 884744 | tf_op jit(solution)/shard_map/while/body/eval_jaxpr/ppermute | solution.py:13
Sparse Core Ops, SparseCore 0:
  11.7 75.2 all-gather.1
  576.1 153.7 all-reduce.4
where the time goes:
time: 741 us; the launch traced here: 738 us
  waiting for transfers between devices  494 us (67%)
  matrix products  138 us (19%)
  starting transfers between devices  59.9 us (8%)
  other arithmetic  22.5 us (3%)
  between operations  15.5 us (2%)
    ppermute x31, waiting for transfers between devices, shifted(): return lax.ppermute(block, axis, route)  269 us
    unnamed x3, waiting for transfers between devices  150 us
    all_gather x1, waiting for transfers between devices, per_device(): block_rows = lax.all_gather(latents, 'seq', axis=0, tiled=True)  75.9 us
    ppermute x31, starting transfers between devices, shifted(): return lax.ppermute(block, axis, route)  59.8 us
    dot_general x33, matrix products, score_block(): lax.dot_general(block_rows, query_rows, (((1,), (1,)), ((), ())), preferr...  42.6 us
    dot_general x32, matrix products, grad_block(): lax.dot_general(dscore, block_rows, (((0,), (0,)), ((), ())), preferred_e...  40.9 us
    dot_general x32, matrix products, grad_block(): lax.dot_general(block_rows[:, :value_width], grad_rows, (((1,), (1,)), ((...  36.5 us
    add x32, other arithmetic, per_device(): query_pos = query_start[0] + lax.iota(jnp.int32, row_count) // head_count  20.1 us
  transfers between devices with their start and end apart: 33, of which 33 were waited for; matrix products, arithmetic and copies ran while one was open for 6% of the time, Pallas kernels for 0%

commit v1 on v0

--- a/solution.py
+++ b/solution.py
@@ -78,7 +78,9 @@
         jnp.full((row_count,), masked_score, jnp.float32),
         jnp.zeros((row_count,), jnp.float32),
     )
-    block_rows = lax.all_gather(latents, "seq", axis=0, tiled=True)
+    block_rows = jnp.concatenate(
+        lax.all_to_all(jnp.stack([latents] * lax.axis_size("seq")), "seq", 0, 0), axis=0
+    )
     running = start_state
     running = norm_step(running, block_rows, jnp.int32(0), query_rows, query_pos)
     add_stored = block_rows

time: 741 us -> 790 us (1.066)
  waiting for transfers between devices: 494 us -> 528 us
  starting transfers between devices: 59.9 us -> 73.2 us
    all_to_all x0 -> x1, waiting for transfers between devices: none -> 107 us  [per_device(): lax.all_to_all(jnp.stack([latents] * lax.axis_size('seq')), 'seq', 0, 0)]
    all_gather x1 -> x0, waiting for transfers between devices: 75.9 us -> none  [per_device(): block_rows = lax.all_gather(latents, 'seq', axis=0, tiled=True)]
    all_to_all x0 -> x1, starting transfers between devices: none -> 13.6 us  [per_device(): lax.all_to_all(jnp.stack([latents] * lax.axis_size('seq')), 'seq', 0, 0)]
    unnamed x3 -> x2, waiting for transfers between devices: 150 us -> 147 us
  transfers between devices with their start and end apart: 33 -> 33, of which waited for: 33 -> 33; matrix products, arithmetic and copies ran while one was open for 6% -> 5% of each run, Pallas kernels for 0% -> 0%
where the time goes in v1:
time: 790 us; the launch traced here: 786 us
  waiting for transfers between devices  528 us (67%)
  matrix products  134 us (17%)
  starting transfers between devices  73.2 us (9%)
  other arithmetic  21.4 us (3%)
  between operations  15.5 us (2%)
  local copies, waits for them, and re-layouts  12.4 us (2%)
    ppermute x31, waiting for transfers between devices, shifted(): return lax.ppermute(block, axis, route)  274 us
    unnamed x2, waiting for transfers between devices  147 us
    all_to_all x1, waiting for transfers between devices, per_device(): lax.all_to_all(jnp.stack([latents] * lax.axis_size('seq')), 'seq', 0, 0)  107 us
    ppermute x31, starting transfers between devices, shifted(): return lax.ppermute(block, axis, route)  59.5 us
    dot_general x33, matrix products, score_block(): lax.dot_general(block_rows, query_rows, (((1,), (1,)), ((), ())), preferr...  41.4 us
    dot_general x32, matrix products, grad_block(): lax.dot_general(dscore, block_rows, (((0,), (0,)), ((), ())), preferred_e...  38.5 us
    dot_general x32, matrix products, grad_block(): lax.dot_general(block_rows[:, :value_width], grad_rows, (((1,), (1,)), ((...  35.8 us
    add x32, other arithmetic, per_device(): query_pos = query_start[0] + lax.iota(jnp.int32, row_count) // head_count  20.1 us
  transfers between devices with their start and end apart: 33, of which 33 were waited for; matrix products, arithmetic and copies ran while one was open for 5% of the time, Pallas kernels for 0%

profile of v1, /device:TPU:2, one launch (start us, length us, event | category | flops | bytes accessed | tf_op | source)
XLA Modules:
  0.0 786.4 jit_solution(217087963814648242)
XLA Ops:
  7.2 4.1 stack.2
  11.3 13.6 %all-to-all-start = ((bf16[32,128,576]{1,2,0:T(8,128)(2,1)}), bf16[32,128,576]{1,2,0:T(8,128)(2,1)}, u32[]{:S(2)}, u32[]{:S(2)}) async-start(bf16[32,128,576]{1,2,0:T(8,128)(2,1)} %stack.2), calls=%async_computation | async-start | bytes 9437184 | tf_op jit(solution)/shard_map/all_to_all | solution.py:82
  26.0 106.9 %all-to-all-done = bf16[32,128,576]{1,2,0:T(8,128)(2,1)} async-done(((bf16[32,128,576]{1,2,0:T(8,128)(2,1)}), bf16[32,128,576]{1,2,0:T(8,128)(2,1)}, u32[]{:S(2)}, u32[]{:S(2)}) %all-to-all-start) | async-done | bytes 4718624 | tf_op jit(solution)/shard_map/all_to_all | solution.py:82
  133.0 4.2 fusion.41
  138.3 3.0 copy_bitcast_fusion
  143.5 482.2 %while.19 = (s32[]{:T(128)}, f32[128,576]{0,1:T(8,128)S(1)}, f32[256,576]{0,1:T(8,128)S(1)}, s32[]{:T(128)}, bf16[4096,576]{0,1:T(8,128)(2,1)}, /*index=5*/bf16[...) while((s32[]{:T(128)}, f32[128,576]{0,1:T(8,128)S(1)}, ...), condition=%wide.wide.region_4.5_spmd.clone, body=%wide.wide.region_3.4_spmd.clone.sunk | while | flops 181127568 | bytes 5608862 | solution.py:106
  147.1 1.9 collective-permute-start
  150.2 4.9 collective-permute-done
  158.7 1.9 collective-permute-start
  161.8 4.9 collective-permute-done
  170.3 1.9 collective-permute-start
  173.5 5.6 collective-permute-done
  182.7 1.9 collective-permute-start
  185.8 10.5 %collective-permute-done = f32[128,576]{0,1:T(8,128)S(1)} collective-permute-done((f32[128,576]{0,1:T(8,128)S(1)}, f32[128,576]{0,1:T(8,128)S(1)}, u32[]{:S(2)}, u32[]{:S(2)}) %collective-permute-start) | collective-permute-done | bytes 294944 | tf_op jit(solution)/shard_map/while/body/eval_jaxpr/ppermute | solution.py:13
  200.0 1.9 collective-permute-start
  203.1 9.1 %collective-permute-done = f32[128,576]{0,1:T(8,128)S(1)} collective-permute-done((f32[128,576]{0,1:T(8,128)S(1)}, f32[128,576]{0,1:T(8,128)S(1)}, u32[]{:S(2)}, u32[]{:S(2)}) %collective-permute-start) | collective-permute-done | bytes 294944 | tf_op jit(solution)/shard_map/while/body/eval_jaxpr/ppermute | solution.py:13
  215.8 1.9 collective-permute-start
  219.0 9.1 %collective-permute-done = f32[128,576]{0,1:T(8,128)S(1)} collective-permute-done((f32[128,576]{0,1:T(8,128)S(1)}, f32[128,576]{0,1:T(8,128)S(1)}, u32[]{:S(2)}, u32[]{:S(2)}) %collective-permute-start) | collective-permute-done | bytes 294944 | tf_op jit(solution)/shard_map/while/body/eval_jaxpr/ppermute | solution.py:13
  231.7 1.9 collective-permute-start
  234.8 9.1 %collective-permute-done = f32[128,576]{0,1:T(8,128)S(1)} collective-permute-done((f32[128,576]{0,1:T(8,128)S(1)}, f32[128,576]{0,1:T(8,128)S(1)}, u32[]{:S(2)}, u32[]{:S(2)}) %collective-permute-start) | collective-permute-done | bytes 294944 | tf_op jit(solution)/shard_map/while/body/eval_jaxpr/ppermute | solution.py:13
  247.5 1.9 collective-permute-start
  250.7 9.1 %collective-permute-done = f32[128,576]{0,1:T(8,128)S(1)} collective-permute-done((f32[128,576]{0,1:T(8,128)S(1)}, f32[128,576]{0,1:T(8,128)S(1)}, u32[]{:S(2)}, u32[]{:S(2)}) %collective-permute-start) | collective-permute-done | bytes 294944 | tf_op jit(solution)/shard_map/while/body/eval_jaxpr/ppermute | solution.py:13
  263.4 1.9 collective-permute-start
  266.5 9.1 %collective-permute-done = f32[128,576]{0,1:T(8,128)S(1)} collective-permute-done((f32[128,576]{0,1:T(8,128)S(1)}, f32[128,576]{0,1:T(8,128)S(1)}, u32[]{:S(2)}, u32[]{:S(2)}) %collective-permute-start) | collective-permute-done | bytes 294944 | tf_op jit(solution)/shard_map/while/body/eval_jaxpr/ppermute | solution.py:13
  279.2 1.9 collective-permute-start
  282.4 9.1 %collective-permute-done = f32[128,576]{0,1:T(8,128)S(1)} collective-permute-done((f32[128,576]{0,1:T(8,128)S(1)}, f32[128,576]{0,1:T(8,128)S(1)}, u32[]{:S(2)}, u32[]{:S(2)}) %collective-permute-start) | collective-permute-done | bytes 294944 | tf_op jit(solution)/shard_map/while/body/eval_jaxpr/ppermute | solution.py:13
  295.1 1.9 collective-permute-start
  298.2 9.1 %collective-permute-done = f32[128,576]{0,1:T(8,128)S(1)} collective-permute-done((f32[128,576]{0,1:T(8,128)S(1)}, f32[128,576]{0,1:T(8,128)S(1)}, u32[]{:S(2)}, u32[]{:S(2)}) %collective-permute-start) | collective-permute-done | bytes 294944 | tf_op jit(solution)/shard_map/while/body/eval_jaxpr/ppermute | solution.py:13
  310.9 1.9 collective-permute-start
  314.0 9.1 %collective-permute-done = f32[128,576]{0,1:T(8,128)S(1)} collective-permute-done((f32[128,576]{0,1:T(8,128)S(1)}, f32[128,576]{0,1:T(8,128)S(1)}, u32[]{:S(2)}, u32[]{:S(2)}) %collective-permute-start) | collective-permute-done | bytes 294944 | tf_op jit(solution)/shard_map/while/body/eval_jaxpr/ppermute | solution.py:13
  326.8 1.9 collective-permute-start
  329.9 9.1 %collective-permute-done = f32[128,576]{0,1:T(8,128)S(1)} collective-permute-done((f32[128,576]{0,1:T(8,128)S(1)}, f32[128,576]{0,1:T(8,128)S(1)}, u32[]{:S(2)}, u32[]{:S(2)}) %collective-permute-start) | collective-permute-done | bytes 294944 | tf_op jit(solution)/shard_map/while/body/eval_jaxpr/ppermute | solution.py:13
  342.6 1.9 collective-permute-start
  345.7 9.1 %collective-permute-done = f32[128,576]{0,1:T(8,128)S(1)} collective-permute-done((f32[128,576]{0,1:T(8,128)S(1)}, f32[128,576]{0,1:T(8,128)S(1)}, u32[]{:S(2)}, u32[]{:S(2)}) %collective-permute-start) | collective-permute-done | bytes 294944 | tf_op jit(solution)/shard_map/while/body/eval_jaxpr/ppermute | solution.py:13
  358.4 1.9 collective-permute-start
  361.6 9.1 %collective-permute-done = f32[128,576]{0,1:T(8,128)S(1)} collective-permute-done((f32[128,576]{0,1:T(8,128)S(1)}, f32[128,576]{0,1:T(8,128)S(1)}, u32[]{:S(2)}, u32[]{:S(2)}) %collective-permute-start) | collective-permute-done | bytes 294944 | tf_op jit(solution)/shard_map/while/body/eval_jaxpr/ppermute | solution.py:13
  374.3 1.9 collective-permute-start
  377.4 9.1 %collective-permute-done = f32[128,576]{0,1:T(8,128)S(1)} collective-permute-done((f32[128,576]{0,1:T(8,128)S(1)}, f32[128,576]{0,1:T(8,128)S(1)}, u32[]{:S(2)}, u32[]{:S(2)}) %collective-permute-start) | collective-permute-done | bytes 294944 | tf_op jit(solution)/shard_map/while/body/eval_jaxpr/ppermute | solution.py:13
  390.1 1.9 collective-permute-start
  393.3 9.2 %collective-permute-done = f32[128,576]{0,1:T(8,128)S(1)} collective-permute-done((f32[128,576]{0,1:T(8,128)S(1)}, f32[128,576]{0,1:T(8,128)S(1)}, u32[]{:S(2)}, u32[]{:S(2)}) %collective-permute-start) | collective-permute-done | bytes 294944 | tf_op jit(solution)/shard_map/while/body/eval_jaxpr/ppermute | solution.py:13
  406.0 1.9 collective-permute-start
  409.2 9.2 %collective-permute-done = f32[128,576]{0,1:T(8,128)S(1)} collective-permute-done((f32[128,576]{0,1:T(8,128)S(1)}, f32[128,576]{0,1:T(8,128)S(1)}, u32[]{:S(2)}, u32[]{:S(2)}) %collective-permute-start) | collective-permute-done | bytes 294944 | tf_op jit(solution)/shard_map/while/body/eval_jaxpr/ppermute | solution.py:13
  422.0 1.9 collective-permute-start
  425.1 9.2 %collective-permute-done = f32[128,576]{0,1:T(8,128)S(1)} collective-permute-done((f32[128,576]{0,1:T(8,128)S(1)}, f32[128,576]{0,1:T(8,128)S(1)}, u32[]{:S(2)}, u32[]{:S(2)}) %collective-permute-start) | collective-permute-done | bytes 294944 | tf_op jit(solution)/shard_map/while/body/eval_jaxpr/ppermute | solution.py:13
  437.9 1.9 collective-permute-start
  441.1 9.2 %collective-permute-done = f32[128,576]{0,1:T(8,128)S(1)} collective-permute-done((f32[128,576]{0,1:T(8,128)S(1)}, f32[128,576]{0,1:T(8,128)S(1)}, u32[]{:S(2)}, u32[]{:S(2)}) %collective-permute-start) | collective-permute-done | bytes 294944 | tf_op jit(solution)/shard_map/while/body/eval_jaxpr/ppermute | solution.py:13
  453.9 1.9 collective-permute-start
  457.0 9.2 %collective-permute-done = f32[128,576]{0,1:T(8,128)S(1)} collective-permute-done((f32[128,576]{0,1:T(8,128)S(1)}, f32[128,576]{0,1:T(8,128)S(1)}, u32[]{:S(2)}, u32[]{:S(2)}) %collective-permute-start) | collective-permute-done | bytes 294944 | tf_op jit(solution)/shard_map/while/body/eval_jaxpr/ppermute | solution.py:13
  469.8 1.9 collective-permute-start
  473.0 9.2 %collective-permute-done = f32[128,576]{0,1:T(8,128)S(1)} collective-permute-done((f32[128,576]{0,1:T(8,128)S(1)}, f32[128,576]{0,1:T(8,128)S(1)}, u32[]{:S(2)}, u32[]{:S(2)}) %collective-permute-start) | collective-permute-done | bytes 294944 | tf_op jit(solution)/shard_map/while/body/eval_jaxpr/ppermute | solution.py:13
  485.8 1.9 collective-permute-start
  488.9 9.2 %collective-permute-done = f32[128,576]{0,1:T(8,128)S(1)} collective-permute-done((f32[128,576]{0,1:T(8,128)S(1)}, f32[128,576]{0,1:T(8,128)S(1)}, u32[]{:S(2)}, u32[]{:S(2)}) %collective-permute-start) | collective-permute-done | bytes 294944 | tf_op jit(solution)/shard_map/while/body/eval_jaxpr/ppermute | solution.py:13
  504.9 9.2 %collective-permute-done = f32[128,576]{0,1:T(8,128)S(1)} collective-permute-done((f32[128,576]{0,1:T(8,128)S(1)}, f32[128,576]{0,1:T(8,128)S(1)}, u32[]{:S(2)}, u32[]{:S(2)}) %collective-permute-start) | collective-permute-done | bytes 294944 | tf_op jit(solution)/shard_map/while/body/eval_jaxpr/ppermute | solution.py:13
  517.7 1.9 collective-permute-start
  520.8 9.2 %collective-permute-done = f32[128,576]{0,1:T(8,128)S(1)} collective-permute-done((f32[128,576]{0,1:T(8,128)S(1)}, f32[128,576]{0,1:T(8,128)S(1)}, u32[]{:S(2)}, u32[]{:S(2)}) %collective-permute-start) | collective-permute-done | bytes 294944 | tf_op jit(solution)/shard_map/while/body/eval_jaxpr/ppermute | solution.py:13
  536.7 9.2 %collective-permute-done = f32[128,576]{0,1:T(8,128)S(1)} collective-permute-done((f32[128,576]{0,1:T(8,128)S(1)}, f32[128,576]{0,1:T(8,128)S(1)}, u32[]{:S(2)}, u32[]{:S(2)}) %collective-permute-start) | collective-permute-done | bytes 294944 | tf_op jit(solution)/shard_map/while/body/eval_jaxpr/ppermute | solution.py:13
  552.7 9.2 %collective-permute-done = f32[128,576]{0,1:T(8,128)S(1)} collective-permute-done((f32[128,576]{0,1:T(8,128)S(1)}, f32[128,576]{0,1:T(8,128)S(1)}, u32[]{:S(2)}, u32[]{:S(2)}) %collective-permute-start) | collective-permute-done | bytes 294944 | tf_op jit(solution)/shard_map/while/body/eval_jaxpr/ppermute | solution.py:13
  565.5 1.9 collective-permute-start
  568.6 9.2 %collective-permute-done = f32[128,576]{0,1:T(8,128)S(1)} collective-permute-done((f32[128,576]{0,1:T(8,128)S(1)}, f32[128,576]{0,1:T(8,128)S(1)}, u32[]{:S(2)}, u32[]{:S(2)}) %collective-permute-start) | collective-permute-done | bytes 294944 | tf_op jit(solution)/shard_map/while/body/eval_jaxpr/ppermute | solution.py:13
  584.6 9.2 %collective-permute-done = f32[128,576]{0,1:T(8,128)S(1)} collective-permute-done((f32[128,576]{0,1:T(8,128)S(1)}, f32[128,576]{0,1:T(8,128)S(1)}, u32[]{:S(2)}, u32[]{:S(2)}) %collective-permute-start) | collective-permute-done | bytes 294944 | tf_op jit(solution)/shard_map/while/body/eval_jaxpr/ppermute | solution.py:13
  600.5 9.2 %collective-permute-done = f32[128,576]{0,1:T(8,128)S(1)} collective-permute-done((f32[128,576]{0,1:T(8,128)S(1)}, f32[128,576]{0,1:T(8,128)S(1)}, u32[]{:S(2)}, u32[]{:S(2)}) %collective-permute-start) | collective-permute-done | bytes 294944 | tf_op jit(solution)/shard_map/while/body/eval_jaxpr/ppermute | solution.py:13
  613.3 1.9 collective-permute-start
  616.5 9.2 %collective-permute-done = f32[128,576]{0,1:T(8,128)S(1)} collective-permute-done((f32[128,576]{0,1:T(8,128)S(1)}, f32[128,576]{0,1:T(8,128)S(1)}, u32[]{:S(2)}, u32[]{:S(2)}) %collective-permute-start) | collective-permute-done | bytes 294944 | tf_op jit(solution)/shard_map/while/body/eval_jaxpr/ppermute | solution.py:13
  630.8 147.4 %all-reduce.5.cloned.1.call-done = f32[128,576]{1,0:T(8,128)} async-done(((f32[128,576]{1,0:T(8,128)}), f32[128,576]{1,0:T(8,128)}) %all-reduce.5.cloned.1.call-update) | async-done | bytes 294928
  (253 shorter events, 166.3 us)
Async XLA Ops:
  11.3 13.7 %copy-start = (bf16[32,8,512]{2,1,0:T(8,128)(2,1)S(1)}, bf16[32,8,512]{2,1,0:T(8,128)(2,1)}, u32[]{:S(2)}) copy-start(bf16[32,8,512]{2,1,0:T(8,128)(2,1)} %param.9) | copy-start | bytes 786436
  11.3 13.7 %copy-start.3 = (bf16[32,8,512]{2,1,0:T(8,128)(2,1)S(1)}, bf16[32,8,512]{2,1,0:T(8,128)(2,1)}, u32[]{:S(2)}) copy-start(bf16[32,8,512]{2,1,0:T(8,128)(2,1)} %param.10) | copy-start | bytes 786436
  11.3 121.7 %copy-start.1 = (bf16[32,8,576]{2,1,0:T(8,128)(2,1)S(1)}, bf16[32,8,576]{2,1,0:T(8,128)(2,1)}, u32[]{:S(2)}) copy-start(bf16[32,8,576]{2,1,0:T(8,128)(2,1)} %param.7) | copy-start | bytes 884740
  11.3 121.7 %all-to-all-start = ((bf16[32,128,576]{1,2,0:T(8,128)(2,1)}), bf16[32,128,576]{1,2,0:T(8,128)(2,1)}, u32[]{:S(2)}, u32[]{:S(2)}) async-start(bf16[32,128,576]{1,2,0:T(8,128)(2,1)} %stack.2), calls=%async_computation | async-start | bytes 9437184 | tf_op jit(solution)/shard_map/all_to_all | solution.py:82
  24.9 753.2 %all-reduce.5.cloned.1.call-start = ((), (), s32[]{:S(2)}) async-start(), calls=%async_computation.1 | async-start | bytes 655360
  25.2 112.0 %copy-start.4 = (f32[32,8]{1,0:T(8,128)}, f32[32,8]{1,0:T(8,128)S(1)}, u32[]{:S(2)}) copy-start(f32[32,8]{1,0:T(8,128)S(1)} %multiply_reduce_fusion) | copy-start | bytes 3076
  141.3 2.1 copy-start.2
  147.1 8.0 %collective-permute-start = (f32[128,576]{0,1:T(8,128)S(1)}, f32[128,576]{0,1:T(8,128)S(1)}, u32[]{:S(2)}, u32[]{:S(2)}) collective-permute-start(f32[128,576]{0,1:T(8,128)S(1)} %fusion.96), channel_id=1, source_target_pairs={{496,0},{0,16},{16,32},{32,48},{48,64},{64,80},{80,96},{96,112},{1... | collective-permute-start | bytes 884744 | tf_op jit(solution)/shard_map/while/body/eval_jaxpr/ppermute | solution.py:13
  158.7 8.0 %collective-permute-start = (f32[128,576]{0,1:T(8,128)S(1)}, f32[128,576]{0,1:T(8,128)S(1)}, u32[]{:S(2)}, u32[]{:S(2)}) collective-permute-start(f32[128,576]{0,1:T(8,128)S(1)} %fusion.96), channel_id=1, source_target_pairs={{496,0},{0,16},{16,32},{32,48},{48,64},{64,80},{80,96},{96,112},{1... | collective-permute-start | bytes 884744 | tf_op jit(solution)/shard_map/while/body/eval_jaxpr/ppermute | solution.py:13
  170.3 8.8 %collective-permute-start = (f32[128,576]{0,1:T(8,128)S(1)}, f32[128,576]{0,1:T(8,128)S(1)}, u32[]{:S(2)}, u32[]{:S(2)}) collective-permute-start(f32[128,576]{0,1:T(8,128)S(1)} %fusion.96), channel_id=1, source_target_pairs={{496,0},{0,16},{16,32},{32,48},{48,64},{64,80},{80,96},{96,112},{1... | collective-permute-start | bytes 884744 | tf_op jit(solution)/shard_map/while/body/eval_jaxpr/ppermute | solution.py:13
  182.7 13.7 %collective-permute-start = (f32[128,576]{0,1:T(8,128)S(1)}, f32[128,576]{0,1:T(8,128)S(1)}, u32[]{:S(2)}, u32[]{:S(2)}) collective-permute-start(f32[128,576]{0,1:T(8,128)S(1)} %fusion.96), channel_id=1, source_target_pairs={{496,0},{0,16},{16,32},{32,48},{48,64},{64,80},{80,96},{96,112},{1... | collective-permute-start | bytes 884744 | tf_op jit(solution)/shard_map/while/body/eval_jaxpr/ppermute | solution.py:13
  200.0 12.3 %collective-permute-start = (f32[128,576]{0,1:T(8,128)S(1)}, f32[128,576]{0,1:T(8,128)S(1)}, u32[]{:S(2)}, u32[]{:S(2)}) collective-permute-start(f32[128,576]{0,1:T(8,128)S(1)} %fusion.96), channel_id=1, source_target_pairs={{496,0},{0,16},{16,32},{32,48},{48,64},{64,80},{80,96},{96,112},{1... | collective-permute-start | bytes 884744 | tf_op jit(solution)/shard_map/while/body/eval_jaxpr/ppermute | solution.py:13
  215.8 12.3 %collective-permute-start = (f32[128,576]{0,1:T(8,128)S(1)}, f32[128,576]{0,1:T(8,128)S(1)}, u32[]{:S(2)}, u32[]{:S(2)}) collective-permute-start(f32[128,576]{0,1:T(8,128)S(1)} %fusion.96), channel_id=1, source_target_pairs={{496,0},{0,16},{16,32},{32,48},{48,64},{64,80},{80,96},{96,112},{1... | collective-permute-start | bytes 884744 | tf_op jit(solution)/shard_map/while/body/eval_jaxpr/ppermute | solution.py:13
  231.7 12.3 %collective-permute-start = (f32[128,576]{0,1:T(8,128)S(1)}, f32[128,576]{0,1:T(8,128)S(1)}, u32[]{:S(2)}, u32[]{:S(2)}) collective-permute-start(f32[128,576]{0,1:T(8,128)S(1)} %fusion.96), channel_id=1, source_target_pairs={{496,0},{0,16},{16,32},{32,48},{48,64},{64,80},{80,96},{96,112},{1... | collective-permute-start | bytes 884744 | tf_op jit(solution)/shard_map/while/body/eval_jaxpr/ppermute | solution.py:13
  247.5 12.3 %collective-permute-start = (f32[128,576]{0,1:T(8,128)S(1)}, f32[128,576]{0,1:T(8,128)S(1)}, u32[]{:S(2)}, u32[]{:S(2)}) collective-permute-start(f32[128,576]{0,1:T(8,128)S(1)} %fusion.96), channel_id=1, source_target_pairs={{496,0},{0,16},{16,32},{32,48},{48,64},{64,80},{80,96},{96,112},{1... | collective-permute-start | bytes 884744 | tf_op jit(solution)/shard_map/while/body/eval_jaxpr/ppermute | solution.py:13
  263.4 12.3 %collective-permute-start = (f32[128,576]{0,1:T(8,128)S(1)}, f32[128,576]{0,1:T(8,128)S(1)}, u32[]{:S(2)}, u32[]{:S(2)}) collective-permute-start(f32[128,576]{0,1:T(8,128)S(1)} %fusion.96), channel_id=1, source_target_pairs={{496,0},{0,16},{16,32},{32,48},{48,64},{64,80},{80,96},{96,112},{1... | collective-permute-start | bytes 884744 | tf_op jit(solution)/shard_map/while/body/eval_jaxpr/ppermute | solution.py:13
  279.2 12.3 %collective-permute-start = (f32[128,576]{0,1:T(8,128)S(1)}, f32[128,576]{0,1:T(8,128)S(1)}, u32[]{:S(2)}, u32[]{:S(2)}) collective-permute-start(f32[128,576]{0,1:T(8,128)S(1)} %fusion.96), channel_id=1, source_target_pairs={{496,0},{0,16},{16,32},{32,48},{48,64},{64,80},{80,96},{96,112},{1... | collective-permute-start | bytes 884744 | tf_op jit(solution)/shard_map/while/body/eval_jaxpr/ppermute | solution.py:13
  295.1 12.3 %collective-permute-start = (f32[128,576]{0,1:T(8,128)S(1)}, f32[128,576]{0,1:T(8,128)S(1)}, u32[]{:S(2)}, u32[]{:S(2)}) collective-permute-start(f32[128,576]{0,1:T(8,128)S(1)} %fusion.96), channel_id=1, source_target_pairs={{496,0},{0,16},{16,32},{32,48},{48,64},{64,80},{80,96},{96,112},{1... | collective-permute-start | bytes 884744 | tf_op jit(solution)/shard_map/while/body/eval_jaxpr/ppermute | solution.py:13
  310.9 12.3 %collective-permute-start = (f32[128,576]{0,1:T(8,128)S(1)}, f32[128,576]{0,1:T(8,128)S(1)}, u32[]{:S(2)}, u32[]{:S(2)}) collective-permute-start(f32[128,576]{0,1:T(8,128)S(1)} %fusion.96), channel_id=1, source_target_pairs={{496,0},{0,16},{16,32},{32,48},{48,64},{64,80},{80,96},{96,112},{1... | collective-permute-start | bytes 884744 | tf_op jit(solution)/shard_map/while/body/eval_jaxpr/ppermute | solution.py:13
  326.8 12.3 %collective-permute-start = (f32[128,576]{0,1:T(8,128)S(1)}, f32[128,576]{0,1:T(8,128)S(1)}, u32[]{:S(2)}, u32[]{:S(2)}) collective-permute-start(f32[128,576]{0,1:T(8,128)S(1)} %fusion.96), channel_id=1, source_target_pairs={{496,0},{0,16},{16,32},{32,48},{48,64},{64,80},{80,96},{96,112},{1... | collective-permute-start | bytes 884744 | tf_op jit(solution)/shard_map/while/body/eval_jaxpr/ppermute | solution.py:13
  342.6 12.3 %collective-permute-start = (f32[128,576]{0,1:T(8,128)S(1)}, f32[128,576]{0,1:T(8,128)S(1)}, u32[]{:S(2)}, u32[]{:S(2)}) collective-permute-start(f32[128,576]{0,1:T(8,128)S(1)} %fusion.96), channel_id=1, source_target_pairs={{496,0},{0,16},{16,32},{32,48},{48,64},{64,80},{80,96},{96,112},{1... | collective-permute-start | bytes 884744 | tf_op jit(solution)/shard_map/while/body/eval_jaxpr/ppermute | solution.py:13
  358.4 12.3 %collective-permute-start = (f32[128,576]{0,1:T(8,128)S(1)}, f32[128,576]{0,1:T(8,128)S(1)}, u32[]{:S(2)}, u32[]{:S(2)}) collective-permute-start(f32[128,576]{0,1:T(8,128)S(1)} %fusion.96), channel_id=1, source_target_pairs={{496,0},{0,16},{16,32},{32,48},{48,64},{64,80},{80,96},{96,112},{1... | collective-permute-start | bytes 884744 | tf_op jit(solution)/shard_map/while/body/eval_jaxpr/ppermute | solution.py:13
  374.3 12.3 %collective-permute-start = (f32[128,576]{0,1:T(8,128)S(1)}, f32[128,576]{0,1:T(8,128)S(1)}, u32[]{:S(2)}, u32[]{:S(2)}) collective-permute-start(f32[128,576]{0,1:T(8,128)S(1)} %fusion.96), channel_id=1, source_target_pairs={{496,0},{0,16},{16,32},{32,48},{48,64},{64,80},{80,96},{96,112},{1... | collective-permute-start | bytes 884744 | tf_op jit(solution)/shard_map/while/body/eval_jaxpr/ppermute | solution.py:13
  390.1 12.3 %collective-permute-start = (f32[128,576]{0,1:T(8,128)S(1)}, f32[128,576]{0,1:T(8,128)S(1)}, u32[]{:S(2)}, u32[]{:S(2)}) collective-permute-start(f32[128,576]{0,1:T(8,128)S(1)} %fusion.96), channel_id=1, source_target_pairs={{496,0},{0,16},{16,32},{32,48},{48,64},{64,80},{80,96},{96,112},{1... | collective-permute-start | bytes 884744 | tf_op jit(solution)/shard_map/while/body/eval_jaxpr/ppermute | solution.py:13
  406.0 12.4 %collective-permute-start = (f32[128,576]{0,1:T(8,128)S(1)}, f32[128,576]{0,1:T(8,128)S(1)}, u32[]{:S(2)}, u32[]{:S(2)}) collective-permute-start(f32[128,576]{0,1:T(8,128)S(1)} %fusion.96), channel_id=1, source_target_pairs={{496,0},{0,16},{16,32},{32,48},{48,64},{64,80},{80,96},{96,112},{1... | collective-permute-start | bytes 884744 | tf_op jit(solution)/shard_map/while/body/eval_jaxpr/ppermute | solution.py:13
  422.0 12.4 %collective-permute-start = (f32[128,576]{0,1:T(8,128)S(1)}, f32[128,576]{0,1:T(8,128)S(1)}, u32[]{:S(2)}, u32[]{:S(2)}) collective-permute-start(f32[128,576]{0,1:T(8,128)S(1)} %fusion.96), channel_id=1, source_target_pairs={{496,0},{0,16},{16,32},{32,48},{48,64},{64,80},{80,96},{96,112},{1... | collective-permute-start | bytes 884744 | tf_op jit(solution)/shard_map/while/body/eval_jaxpr/ppermute | solution.py:13
  437.9 12.4 %collective-permute-start = (f32[128,576]{0,1:T(8,128)S(1)}, f32[128,576]{0,1:T(8,128)S(1)}, u32[]{:S(2)}, u32[]{:S(2)}) collective-permute-start(f32[128,576]{0,1:T(8,128)S(1)} %fusion.96), channel_id=1, source_target_pairs={{496,0},{0,16},{16,32},{32,48},{48,64},{64,80},{80,96},{96,112},{1... | collective-permute-start | bytes 884744 | tf_op jit(solution)/shard_map/while/body/eval_jaxpr/ppermute | solution.py:13
  453.9 12.4 %collective-permute-start = (f32[128,576]{0,1:T(8,128)S(1)}, f32[128,576]{0,1:T(8,128)S(1)}, u32[]{:S(2)}, u32[]{:S(2)}) collective-permute-start(f32[128,576]{0,1:T(8,128)S(1)} %fusion.96), channel_id=1, source_target_pairs={{496,0},{0,16},{16,32},{32,48},{48,64},{64,80},{80,96},{96,112},{1... | collective-permute-start | bytes 884744 | tf_op jit(solution)/shard_map/while/body/eval_jaxpr/ppermute | solution.py:13
  469.8 12.4 %collective-permute-start = (f32[128,576]{0,1:T(8,128)S(1)}, f32[128,576]{0,1:T(8,128)S(1)}, u32[]{:S(2)}, u32[]{:S(2)}) collective-permute-start(f32[128,576]{0,1:T(8,128)S(1)} %fusion.96), channel_id=1, source_target_pairs={{496,0},{0,16},{16,32},{32,48},{48,64},{64,80},{80,96},{96,112},{1... | collective-permute-start | bytes 884744 | tf_op jit(solution)/shard_map/while/body/eval_jaxpr/ppermute | solution.py:13
  485.8 12.4 %collective-permute-start = (f32[128,576]{0,1:T(8,128)S(1)}, f32[128,576]{0,1:T(8,128)S(1)}, u32[]{:S(2)}, u32[]{:S(2)}) collective-permute-start(f32[128,576]{0,1:T(8,128)S(1)} %fusion.96), channel_id=1, source_target_pairs={{496,0},{0,16},{16,32},{32,48},{48,64},{64,80},{80,96},{96,112},{1... | collective-permute-start | bytes 884744 | tf_op jit(solution)/shard_map/while/body/eval_jaxpr/ppermute | solution.py:13
  501.7 12.4 %collective-permute-start = (f32[128,576]{0,1:T(8,128)S(1)}, f32[128,576]{0,1:T(8,128)S(1)}, u32[]{:S(2)}, u32[]{:S(2)}) collective-permute-start(f32[128,576]{0,1:T(8,128)S(1)} %fusion.96), channel_id=1, source_target_pairs={{496,0},{0,16},{16,32},{32,48},{48,64},{64,80},{80,96},{96,112},{1... | collective-permute-start | bytes 884744 | tf_op jit(solution)/shard_map/while/body/eval_jaxpr/ppermute | solution.py:13
  517.7 12.4 %collective-permute-start = (f32[128,576]{0,1:T(8,128)S(1)}, f32[128,576]{0,1:T(8,128)S(1)}, u32[]{:S(2)}, u32[]{:S(2)}) collective-permute-start(f32[128,576]{0,1:T(8,128)S(1)} %fusion.96), channel_id=1, source_target_pairs={{496,0},{0,16},{16,32},{32,48},{48,64},{64,80},{80,96},{96,112},{1... | collective-permute-start | bytes 884744 | tf_op jit(solution)/shard_map/while/body/eval_jaxpr/ppermute | solution.py:13
  533.6 12.4 %collective-permute-start = (f32[128,576]{0,1:T(8,128)S(1)}, f32[128,576]{0,1:T(8,128)S(1)}, u32[]{:S(2)}, u32[]{:S(2)}) collective-permute-start(f32[128,576]{0,1:T(8,128)S(1)} %fusion.96), channel_id=1, source_target_pairs={{496,0},{0,16},{16,32},{32,48},{48,64},{64,80},{80,96},{96,112},{1... | collective-permute-start | bytes 884744 | tf_op jit(solution)/shard_map/while/body/eval_jaxpr/ppermute | solution.py:13
  549.5 12.4 %collective-permute-start = (f32[128,576]{0,1:T(8,128)S(1)}, f32[128,576]{0,1:T(8,128)S(1)}, u32[]{:S(2)}, u32[]{:S(2)}) collective-permute-start(f32[128,576]{0,1:T(8,128)S(1)} %fusion.96), channel_id=1, source_target_pairs={{496,0},{0,16},{16,32},{32,48},{48,64},{64,80},{80,96},{96,112},{1... | collective-permute-start | bytes 884744 | tf_op jit(solution)/shard_map/while/body/eval_jaxpr/ppermute | solution.py:13
  565.5 12.4 %collective-permute-start = (f32[128,576]{0,1:T(8,128)S(1)}, f32[128,576]{0,1:T(8,128)S(1)}, u32[]{:S(2)}, u32[]{:S(2)}) collective-permute-start(f32[128,576]{0,1:T(8,128)S(1)} %fusion.96), channel_id=1, source_target_pairs={{496,0},{0,16},{16,32},{32,48},{48,64},{64,80},{80,96},{96,112},{1... | collective-permute-start | bytes 884744 | tf_op jit(solution)/shard_map/while/body/eval_jaxpr/ppermute | solution.py:13
  581.4 12.4 %collective-permute-start = (f32[128,576]{0,1:T(8,128)S(1)}, f32[128,576]{0,1:T(8,128)S(1)}, u32[]{:S(2)}, u32[]{:S(2)}) collective-permute-start(f32[128,576]{0,1:T(8,128)S(1)} %fusion.96), channel_id=1, source_target_pairs={{496,0},{0,16},{16,32},{32,48},{48,64},{64,80},{80,96},{96,112},{1... | collective-permute-start | bytes 884744 | tf_op jit(solution)/shard_map/while/body/eval_jaxpr/ppermute | solution.py:13
  597.4 12.4 %collective-permute-start = (f32[128,576]{0,1:T(8,128)S(1)}, f32[128,576]{0,1:T(8,128)S(1)}, u32[]{:S(2)}, u32[]{:S(2)}) collective-permute-start(f32[128,576]{0,1:T(8,128)S(1)} %fusion.96), channel_id=1, source_target_pairs={{496,0},{0,16},{16,32},{32,48},{48,64},{64,80},{80,96},{96,112},{1... | collective-permute-start | bytes 884744 | tf_op jit(solution)/shard_map/while/body/eval_jaxpr/ppermute | solution.py:13
  613.3 12.4 %collective-permute-start = (f32[128,576]{0,1:T(8,128)S(1)}, f32[128,576]{0,1:T(8,128)S(1)}, u32[]{:S(2)}, u32[]{:S(2)}) collective-permute-start(f32[128,576]{0,1:T(8,128)S(1)} %fusion.96), channel_id=1, source_target_pairs={{496,0},{0,16},{16,32},{32,48},{48,64},{64,80},{80,96},{96,112},{1... | collective-permute-start | bytes 884744 | tf_op jit(solution)/shard_map/while/body/eval_jaxpr/ppermute | solution.py:13
Sparse Core Ops, SparseCore 0:
  626.9 151.2 all-reduce.4
